TPU v7x, 256 devices: a whole 4x4x8 slice. The times are simulated.
256 devices in a mesh: tm: 64 (over z, x, core), space: 4 (over y).
Axes of the slice: x: 4, y: 4, z: 8, core: 2. Of those that a mesh axis runs over, the one named last changes fastest.
Arguments:
- frames: bfloat16 [256, 32, 256, 128], P('tm', 'space'), may hold values from -8 to 8
- conv_weight: bfloat16 [3, 1152, 128], replicated, may hold values from -0.109375 to 0.109375
- norm_gain: float32 [128], replicated, may hold values from 0.1 to 1.9
- norm_shift: float32 [128], replicated, may hold values from -3 to 3
- clip_lengths: int32 [32], replicated, may hold values from 1 to 64, 256 in all
Outputs:
- encoded: bfloat16 [256, 32, 256, 128], P('tm', 'space')
Inputs may be any that keep to these rules, and one draw needn't show every extreme that they name: `clip_lengths`: clips are packed end to end and fill all 256 frames; the longest has exactly 64 frames.
All inputs are finite; a program needn't handle non-finite values.
Results may differ from a plain program's by a relative error of at most 0.00065.
Values may be sent and summed in bfloat16 or wider, within the bound.
A program may use at most 192 MiB of HBM per device.

v0:
```python
import jax
import jax.numpy as jnp
from jax import lax
from jax.sharding import PartitionSpec as P

GROUPS = 32


def from_behind(block, axis, distance):
    devices = range(lax.axis_size(axis))
    route = [(i - distance, i) for i in devices if i - distance in devices]
    return lax.ppermute(block, axis, route)


def extended_2(cells, sides, width):
    for axis, dim in sides:
        count = lax.axis_size(axis)
        ends = count - 1
        head = lax.slice_in_dim(cells, 0, width, axis=dim)
        tail = lax.slice_in_dim(cells, cells.shape[dim] - width, cells.shape[dim], axis=dim)
        cells = jnp.concatenate(
            [
                lax.ppermute(tail, axis, [(i, (i + 1) % count) for i in range(ends)]),
                cells,
                lax.ppermute(head, axis, [((i + 1) % count, i) for i in range(ends)]),
            ],
            axis=dim,
        )
    return cells


def patches_of(source, band_rows, columns):
    pieces = []
    for row_off in range(3):
        for col_off in range(3):
            pieces.append(source[:, row_off : row_off + band_rows, col_off : col_off + columns, :])
    return jnp.concatenate(pieces, axis=-1)


def clip_index(positions, clip_ends):
    found = jnp.sum((clip_ends[None, :] <= positions[:, None]).astype(jnp.int32), axis=1)
    return jnp.where(positions >= 0, found, -1)


def shards(frames, conv_weight, norm_gain, norm_shift, clip_lengths):
    count_frames, band_rows, columns, channels = frames.shape
    clip_count = clip_lengths.shape[0]
    per_group = channels // GROUPS
    start_frame = lax.axis_index("tm") * count_frames
    clip_ends = jnp.cumsum(clip_lengths)
    positions = start_frame + jnp.arange(count_frames, dtype=jnp.int32)
    clip_here = clip_index(positions, clip_ends)
    earlier = from_behind(frames[count_frames - 2 :], "tm", 1)
    extended = jnp.concatenate([earlier, frames], axis=0)
    rimmed = extended_2(extended, (("space", 1),), 1)
    padded = jnp.pad(rimmed, ((0, 0), (0, 0), (1, 1), (0, 0)))
    patches = patches_of(padded, band_rows, columns)
    running = jnp.zeros((count_frames, band_rows * columns, channels), jnp.float32)
    for step_back in range(3):
        window = patches[2 - step_back : 2 - step_back + count_frames].reshape(
            count_frames * band_rows * columns, 9 * channels
        )
        product = jnp.dot(window, conv_weight[step_back], preferred_element_type=jnp.float32)
        within = (clip_index(positions - step_back, clip_ends) == clip_here).astype(jnp.float32)
        running = running + within[:, None, None] * product.reshape(
            count_frames, band_rows * columns, channels
        )
    conv = running.reshape(count_frames, band_rows, columns, channels)
    onehot = (clip_here[:, None] == jnp.arange(clip_count, dtype=jnp.int32)[None, :]).astype(
        jnp.float32
    )
    counts = clip_lengths.astype(jnp.float32) * float(
        band_rows * lax.axis_size("space") * columns * per_group
    )

    def partial_stat(values):
        frame_sums = jnp.sum(values, axis=(1, 2))
        clip_sums = jnp.dot(onehot.T, frame_sums, precision=lax.Precision.HIGHEST)
        return jnp.sum(clip_sums.reshape(clip_count, GROUPS, per_group), axis=-1)

    def spread(table):
        frame_table = jnp.dot(onehot, table, precision=lax.Precision.HIGHEST)
        return jnp.repeat(frame_table, per_group, axis=1)[:, None, None, :]

    average = lax.psum(partial_stat(conv), ("tm", "space")) / counts[:, None]
    centered = conv - spread(average)
    variance = lax.psum(partial_stat(centered * centered), ("tm", "space")) / counts[:, None]
    normed = centered * spread(lax.rsqrt(variance + 1e-06)) * norm_gain + norm_shift
    return jax.nn.silu(normed).astype(jnp.bfloat16)


def solution(mesh):
    return jax.shard_map(
        shards,
        mesh=mesh,
        in_specs=(P("tm", "space", None, None), P(), P(), P(), P()),
        out_specs=P("tm", "space", None, None),
        check_vma=False,
    )
```

profile of v0, /device:TPU:64, one launch (start us, length us, event | category | flops | bytes accessed | tf_op | source)
XLA Modules:
  0.0 280.4 jit_solution(15145173647037914365)
XLA Ops:
  0.0 0.0 copy-start
  0.0 2.4 slice.57
  2.4 1.9 collective-permute-start
  4.4 0.7 copy.8
  5.1 0.1 reduce-window.8
  5.2 0.1 reduce.2
  5.3 0.2 convert_reduce_fusion.2
  5.5 0.7 convert_multiply_fusion
  6.2 14.7 %collective-permute-done = bf16[2,8,256,128]{3,2,1,0:T(8,128)(2,1)S(1)} collective-permute-done((bf16[2,8,256,128]{3,2,1,0:T(8,128)(2,1)}, bf16[2,8,256,128]{3,2,1,0:T(8,128)(2,1)S(1)}, u32[]{:S(2)}, u32[]{:S(2)}) %collective-permute-start) | collective-permute-done | bytes 1048608 | tf_op jit(solution)/shard_map/ppermute | solution.py:12
  20.9 0.1 constant_dynamic-update-slice_fusion.1
  21.0 0.0 copy-done
  21.0 0.3 constant_dynamic-update-slice_fusion
  21.2 0.1 fusion.34
  21.3 3.5 %collective-permute-start.1 = (bf16[6,1,256,128]{3,2,1,0:T(8,128)(2,1)S(1)}, bf16[6,1,256,128]{3,2,1,0:T(8,128)(2,1)S(1)}, u32[]{:S(2)}, u32[]{:S(2)}) collective-permute-start(bf16[6,1,256,128]{3,2,1,0:T(8,128)(2,1)S(1)} %get-tuple-element.11), channel_id=1, source_target_pairs={{0,1},{1,2},{2,3},{4,5},{5,6},{6,7},{8,9},{9,10},{10,11},{12,13},{... | collective-permute-start | bytes 1179656 | tf_op jit(solution)/shard_map/ppermute | solution.py:23
  24.8 1.3 collective-permute-start.2
  26.2 4.3 %collective-permute-done.1 = bf16[6,1,256,128]{3,2,1,0:T(8,128)(2,1)S(1)} collective-permute-done((bf16[6,1,256,128]{3,2,1,0:T(8,128)(2,1)S(1)}, bf16[6,1,256,128]{3,2,1,0:T(8,128)(2,1)S(1)}, u32[]{:S(2)}, u32[]{:S(2)}) %collective-permute-start.1) | collective-permute-done | bytes 393248 | tf_op jit(solution)/shard_map/ppermute | solution.py:23
  30.4 4.1 %collective-permute-done.2 = bf16[6,1,256,128]{3,2,1,0:T(8,128)(2,1)S(1)} collective-permute-done((bf16[6,1,256,128]{3,2,1,0:T(8,128)(2,1)S(1)}, bf16[6,1,256,128]{3,2,1,0:T(8,128)(2,1)S(1)}, u32[]{:S(2)}, u32[]{:S(2)}) %collective-permute-start.2) | collective-permute-done | bytes 393248 | tf_op jit(solution)/shard_map/ppermute | solution.py:25
  34.6 1.7 fusion.5
  36.3 2.2 slice_dynamic-update-slice_fusion.5
  38.4 2.0 fusion.7
  40.4 2.9 %slice_dynamic-update-slice_fusion.4 = bf16[6,8,256,1152]{3,2,1,0:T(8,128)(2,1)} fusion(bf16[6,8,256,1152]{3,2,1,0:T(8,128)(2,1)} %fusion.7, bf16[6,10,258,128]{3,2,1,0:T(8,128)(2,1)S(1)} %fusion.5), kind=kLoop, calls=%fused_computation.17 | loop fusion | bytes 6291456
  43.4 2.3 slice_dynamic-update-slice_fusion.3
  45.6 1.2 constant_dynamic-update-slice_fusion.3
  46.8 1.5 constant_dynamic-update-slice_fusion.2
  48.3 2.9 %slice_dynamic-update-slice_fusion.2 = bf16[6,8,256,1152]{3,2,1,0:T(8,128)(2,1)} fusion(bf16[6,8,256,1152]{3,2,1,0:T(8,128)(2,1)} %constant_dynamic-update-slice_fusion.2, bf16[6,10,258,128]{3,2,1,0:T(8,128)(2,1)S(1)} %fusion.5), kind=kLoop, calls=%fused_computation.15 | loop fusion | bytes 6291456
  51.2 2.2 slice_dynamic-update-slice_fusion.1
  53.4 1.9 fusion.6
  55.4 2.8 %slice_dynamic-update-slice_fusion = bf16[6,8,256,1152]{3,2,1,0:T(8,128)(2,1)} fusion(bf16[6,8,256,1152]{3,2,1,0:T(8,128)(2,1)} %fusion.6, bf16[6,10,258,128]{3,2,1,0:T(8,128)(2,1)S(1)} %fusion.5), kind=kLoop, calls=%fused_computation.11 | loop fusion | bytes 6291456 | tf_op jit(solution)/shard_map/concatenate | solution.py:37
  58.2 0.0 copy-start.1
  58.2 33.7 %fusion.33 = (bf16[4,8,256,1152]{3,2,1,0:T(8,128)(2,1)S(1)}, bf16[4,8,256,1152]{3,2,1,0:T(8,128)(2,1)}, bf16[4,8,256,1152]{3,2,1,0:T(8,128)(2,1)}) fusion(bf16[6,8,256,1152]{3,2,1,0:T(8,128)(2,1)} %slice_dynamic-update-slice_fusion), kind=kLoop, calls=%fused_computation.63 | loop fusion | bytes 113246208 | tf_op jit(solution)/shard_map/slice | solution.py:60
  91.9 0.0 copy-done.1
  91.9 10.3 %fusion.11 = f32[4,2048,128]{2,1,0:T(8,128)} fusion(bf16[4,2048,1152]{2,1,0:T(8,128)(2,1)} %bitcast.36, bf16[3,1152,128]{2,1,0:T(8,128)(2,1)S(1)} %copy-done.1), kind=kOutput, calls=%fused_computation.26 | convolution fusion | flops 2415919104 | bytes 23363584 | tf_op jit(solution)/shard_map/dot_general | solution.py:63
  102.3 10.3 %fusion.9 = f32[4,2048,128]{2,1,0:T(8,128)} fusion(bf16[4,2048,1152]{2,1,0:T(8,128)(2,1)} %bitcast.35, bf16[3,1152,128]{2,1,0:T(8,128)(2,1)S(1)} %copy-done.1), kind=kOutput, calls=%fused_computation.24 | convolution fusion | flops 2415919104 | bytes 23363584 | tf_op jit(solution)/shard_map/dot_general | solution.py:63
  112.6 9.0 %fusion.35 = (f32[4,128]{1,0:T(4,128)S(1)}, f32[4,2048,128]{2,1,0:T(8,128)}) fusion(bf16[4,2048,1152]{2,1,0:T(8,128)(2,1)S(1)} %bitcast.34, bf16[3,1152,128]{2,1,0:T(8,128)(2,1)S(1)} %copy-done.1, f32[4]{0:T(128)S(1)} %get-tuple-element.14, f32[4,2048,128]{2,1,0:T(8,128)} %fusion.11, f32[4,2048,128]{2,1,0:T(8,128)} %fusion.9, f32[4]{0:T(128)S(1)} %get-tuple-element.13), kind=kOutput, calls=%fused_computation.65 | convolution fusion | flops 2421161472 | bytes 31755264 | tf_op jit(solution)/shard_map/dot_general | solution.py:63
  121.6 0.0 copy-start.2
  121.6 0.0 copy-start.3
  121.6 0.1 dot_general.42
  121.7 0.1 copy.9
  121.8 0.3 convolution_reduce_fusion.1
  122.1 75.6 %psum.14 = f32[32,32]{1,0:T(8,128)S(1)} all-reduce(f32[32,32]{1,0:T(8,128)S(1)} %convolution_reduce_fusion.1), channel_id=1, replica_groups=mesh['tm'=64,'space'=4] {'tm','space'}, use_global_device_ids=true, to_apply=%region_6.7 | all-reduce | flops 1024 | bytes 8192 | tf_op jit(solution)/shard_map/psum | solution.py:85
  197.7 0.2 fusion.20
  197.9 0.1 broadcast_in_dim.9
  198.0 0.1 sub.23
  198.1 2.6 multiply_reduce_fusion
  200.7 0.1 dot_general.46
  200.8 0.1 copy.10
  200.9 0.3 convolution_reduce_fusion
  201.2 73.9 %psum.15 = f32[32,32]{1,0:T(8,128)S(1)} all-reduce(f32[32,32]{1,0:T(8,128)S(1)} %convolution_reduce_fusion), channel_id=1, replica_groups=mesh['tm'=64,'space'=4] {'tm','space'}, use_global_device_ids=true, to_apply=%region_9.10 | all-reduce | flops 1024 | bytes 8192 | tf_op jit(solution)/shard_map/psum | solution.py:87
  275.1 0.2 fusion.16
  275.3 0.1 broadcast_in_dim.10
  275.4 0.1 mul.63
  275.6 0.0 copy-done.2
  275.6 0.0 copy-done.3
  275.6 4.9 %multiply_convert_fusion = bf16[4,8,256,128]{3,2,1,0:T(8,128)(2,1)} fusion(f32[4,8,256,128]{3,2,1,0:T(8,128)} %bitcast.37, f32[128]{0:T(128)S(1)} %copy-done.2, f32[128]{0:T(128)S(1)} %copy-done.3, f32[4,128]{1,0:T(4,128)S(1)} %mul.63, f32[4,128]{1,0:T(4,128)S(1)} %sub.23), kind=kLoop, calls=%fused_computation.6 | loop fusion | flops 9437184 | bytes 6296576 | tf_op jit(solution)/shard_map/convert_element_type | solution.py:89
  (4 shorter events, 0.0 us)
Async XLA Ops:
  0.0 21.0 %copy-start = (bf16[4,8,256,128]{3,2,1,0:T(8,128)(2,1)S(1)}, bf16[4,8,256,128]{3,2,1,0:T(8,128)(2,1)}, u32[]{:S(2)}) copy-start(bf16[4,8,256,128]{3,2,1,0:T(8,128)(2,1)} %param.5) | copy-start | bytes 6291460
  2.4 18.4 %collective-permute-start = (bf16[2,8,256,128]{3,2,1,0:T(8,128)(2,1)}, bf16[2,8,256,128]{3,2,1,0:T(8,128)(2,1)S(1)}, u32[]{:S(2)}, u32[]{:S(2)}) collective-permute-start(bf16[2,8,256,128]{3,2,1,0:T(8,128)(2,1)} %slice.57), channel_id=1, source_target_pairs={{0,4},{4,8},{8,12},{12,16},{16,20},{20,24},{24,28},{28,32},{32,36}... | collective-permute-start | bytes 3145736 | tf_op jit(solution)/shard_map/ppermute | solution.py:12
  21.3 9.1 %collective-permute-start.1 = (bf16[6,1,256,128]{3,2,1,0:T(8,128)(2,1)S(1)}, bf16[6,1,256,128]{3,2,1,0:T(8,128)(2,1)S(1)}, u32[]{:S(2)}, u32[]{:S(2)}) collective-permute-start(bf16[6,1,256,128]{3,2,1,0:T(8,128)(2,1)S(1)} %get-tuple-element.11), channel_id=1, source_target_pairs={{0,1},{1,2},{2,3},{4,5},{5,6},{6,7},{8,9},{9,10},{10,11},{12,13},{... | collective-permute-start | bytes 1179656 | tf_op jit(solution)/shard_map/ppermute | solution.py:23
  24.8 9.8 %collective-permute-start.2 = (bf16[6,1,256,128]{3,2,1,0:T(8,128)(2,1)S(1)}, bf16[6,1,256,128]{3,2,1,0:T(8,128)(2,1)S(1)}, u32[]{:S(2)}, u32[]{:S(2)}) collective-permute-start(bf16[6,1,256,128]{3,2,1,0:T(8,128)(2,1)S(1)} %get-tuple-element.12), channel_id=1, source_target_pairs={{1,0},{2,1},{3,2},{5,4},{6,5},{7,6},{9,8},{10,9},{11,10},{13,12},{... | collective-permute-start | bytes 1179656 | tf_op jit(solution)/shard_map/ppermute | solution.py:25
  58.2 33.7 %copy-start.1 = (bf16[3,1152,128]{2,1,0:T(8,128)(2,1)S(1)}, bf16[3,1152,128]{2,1,0:T(8,128)(2,1)}, u32[]{:S(2)}) copy-start(bf16[3,1152,128]{2,1,0:T(8,128)(2,1)} %param.6) | copy-start | bytes 2654212
  121.6 154.0 %copy-start.2 = (f32[128]{0:T(128)S(1)}, f32[128]{0:T(128)}, u32[]{:S(2)}) copy-start(f32[128]{0:T(128)} %param.8) | copy-start | bytes 1540
  121.6 154.0 %copy-start.3 = (f32[128]{0:T(128)S(1)}, f32[128]{0:T(128)}, u32[]{:S(2)}) copy-start(f32[128]{0:T(128)} %param.7) | copy-start | bytes 1540
where the time goes:
time: 284 us; the launch traced here: 280 us
  blocking collectives  150 us (53%)
  local copies, waits for them, and re-layouts  56.2 us (20%)
  matrix products  30.6 us (11%)
  waiting for transfers between devices  23.1 us (8%)
  other arithmetic  14.2 us (5%)
  starting transfers between devices  6.7 us (2%)
    psum x1, blocking collectives, shards(): average = lax.psum(partial_stat(conv), ('tm', 'space')) / counts[:, None]  75.6 us
    psum x1, blocking collectives, shards(): lax.psum(partial_stat(centered * centered), ('tm', 'space'))  73.9 us
    slice x1, local copies, waits for them, and re-layouts, shards(): patches[2 - step_back:2 - step_back + count_frames]  33.7 us
    dot_general x3, matrix products, shards(): jnp.dot(window, conv_weight[step_back], preferred_element_type=jnp.float32)  29.6 us
    unnamed x16, local copies, waits for them, and re-layouts  15.3 us
    ppermute x1, waiting for transfers between devices, from_behind(): return lax.ppermute(block, axis, route)  14.7 us
  transfers between devices with their start and end apart: 3, of which 3 were waited for; matrix products, arithmetic and copies ran while one was open for 1% of the time, Pallas kernels for 0%

commit v1 on v0

v1 whole, which is shorter than its diff:
```python
import functools

import jax
import jax.numpy as jnp
from jax import lax
from jax.experimental import pallas as pl
from jax.experimental.pallas import tpu as pltpu
from jax.sharding import PartitionSpec as P

GROUPS = 32
MESH = pl.DeviceIdType.MESH
T, S, NX, NZ = 64, 4, 4, 8
FR, ROWS, COLS, CH = 4, 8, 256, 128
BF, F32 = jnp.bfloat16, jnp.float32


def shifted(v):
    z = jnp.zeros((1, CH), v.dtype)
    left = jnp.concatenate([z, v[: COLS - 1]], axis=0)
    right = jnp.concatenate([v[1:], z], axis=0)
    return jnp.concatenate([left, v, right], axis=1)


def group_sum(x):
    lane = lax.broadcasted_iota(jnp.int32, x.shape, 1)
    n = x.shape[1]
    x = x + jnp.where(lane % 2 == 0, pltpu.roll(x, n - 1, 1), pltpu.roll(x, 1, 1))
    return x + jnp.where(lane % 4 < 2, pltpu.roll(x, n - 2, 1), pltpu.roll(x, 2, 1))


def conv_kernel(x, w, lens, acc, tab, XL, XH, YU, YD, PA, W, sS, sQ, st, ct, buf1, buf2,
                lsem, wsem, xsem_s, xsem_r, ysem_s, ysem_r, s1_s, s1_r, s2_s, s2_r):
    t = lax.axis_index("tm")
    y = lax.axis_index("space")
    core = t % 2
    chip = t // 2
    cx = chip % NX
    cz = chip // NX

    def dev(z_, x_, c_, y_):
        return ((z_ * NX + x_) * 2 + c_, y_)

    nxt = ((t + 1) % T, y)
    up = (t, (y + 1) % S)
    down = (t, (y + S - 1) % S)

    near = [(dc, dy) for dc in range(2) for dy in range(S) if (dc, dy) != (0, 0)]
    far = [(dz, dx) for dz in (2, -2, 1, -1, 0) for dx in (2, 1, 3, 0) if (dz, dx) != (0, 0)]
    barrier = pltpu.get_barrier_semaphore()

    def greet(d):
        pl.semaphore_signal(barrier, inc=1, device_id=d, device_id_type=MESH)

    greet(((t + 2 * core - 1 + T) % T, y))

    def near_dev(dc, dy):
        return dev(cz, cx, (core + dc) % 2, (y + dy) % S)

    def far_dev(dz, dx):
        return dev((cz + dz + NZ) % NZ, (cx + dx) % NX, core, y)

    for dc, dy in near:
        greet(near_dev(dc, dy))
    for dz, dx in far:
        greet(far_dev(dz, dx))

    loads = [pltpu.make_async_copy(x.at[f], XL.at[f], lsem.at[f]) for f in range(FR)]
    wloads = []
    for lag in range(3):
        wloads.append(pltpu.make_async_copy(w.at[lag], W.at[lag, pl.ds(0, 1152), pl.ds(0, 128)], wsem.at[lag]))
        wloads.append(pltpu.make_async_copy(w.at[lag], W.at[lag, pl.ds(384, 1152), pl.ds(128, 128)], wsem.at[3 + lag]))
    for c in loads + wloads:
        c.start()

    pl.semaphore_wait(barrier, 1 + len(near) + len(far))

    def rcopy(src, dst, ss, rs, d):
        return pltpu.make_async_remote_copy(src_ref=src, dst_ref=dst, send_sem=ss, recv_sem=rs, device_id=d, device_id_type=MESH)

    xc = []
    for i, (r0, n) in enumerate([(0, 1), (7, 1), (1, 2), (3, 2), (5, 2)]):
        xc.append(rcopy(x.at[pl.ds(2, 2), pl.ds(r0, n)], XH.at[:, pl.ds(r0, n)], xsem_s.at[i], xsem_r.at[i], nxt))
    yc = [
        rcopy(x.at[:, 7], YU.at[pl.ds(2, 4)], ysem_s.at[0], ysem_r.at[0], up),
        rcopy(x.at[:, 0], YD.at[pl.ds(2, 4)], ysem_s.at[1], ysem_r.at[1], down),
        rcopy(XH.at[:, 7], YU.at[pl.ds(0, 2)], ysem_s.at[2], ysem_r.at[2], up),
        rcopy(XH.at[:, 0], YD.at[pl.ds(0, 2)], ysem_s.at[3], ysem_r.at[3], down),
    ]
    xc[0].start()
    xc[1].start()
    yc[0].start()
    yc[1].start()
    xc[2].start()
    xc[3].start()
    xc[4].start()

    pos = [t * FR + i for i in range(FR)]

    def bounds(k, c):
        cum, starts, ends = c
        after = cum + lens[k]
        inside = [(cum <= p) & (p < after) for p in pos]
        starts = tuple(jnp.where(i, cum, s) for i, s in zip(inside, starts))
        ends = tuple(jnp.where(i, after, e) for i, e in zip(inside, ends))
        return after, starts, ends

    zero = jnp.int32(0)
    _, starts, ends = lax.fori_loop(0, 32, bounds, (zero, (zero,) * FR, (zero,) * FR))
    within = [[jnp.where(pos[i] - lag >= starts[i], 1.0, 0.0).astype(F32) for lag in range(3)] for i in range(FR)]

    for lag in range(3):
        W[lag, 1152:1536, 0:128] = jnp.zeros((384, 128), BF)
        W[lag, 0:384, 128:256] = jnp.zeros((384, 128), BF)

    for f in range(FR):
        loads[f].wait()

        def pairs(p, _, f=f):
            PA[f + 2, p, :, 0:384] = shifted(XL[f, 2 * p - 1])
            PA[f + 2, p, :, 384:768] = shifted(XL[f, 2 * p])
            return 0

        lax.fori_loop(1, 4, pairs, 0)
        PA[f + 2, 0, :, 384:768] = shifted(XL[f, 0])
        PA[f + 2, 4, :, 0:384] = shifted(XL[f, 7])
    for c in wloads:
        c.wait()

    def dot(a, b):
        return jnp.dot(a, b, preferred_element_type=F32)

    def local(i, lag):
        a = PA[i + 2 - lag, 1:4].reshape(768, 768)
        d1 = dot(a, W[lag, 768:1536]).reshape(3, 256, 256)
        d0 = dot(a, W[lag, 0:768]).reshape(3, 256, 256)
        return d1, d0

    for i in range(FR):
        d1, d0 = local(i, 0)
        acc[i, 0] = d1[0]
        acc[i, 1] = d1[1] + d0[0]
        acc[i, 2] = d1[2] + d0[1]
        acc[i, 3] = d0[2]
        for lag in range(1, min(i, 2) + 1):
            d1, d0 = local(i, lag)
            s = within[i][lag]
            acc[i, 0] += s * d1[0]
            acc[i, 1] += s * (d1[1] + d0[0])
            acc[i, 2] += s * (d1[2] + d0[1])
            acc[i, 3] += s * d0[2]
        if i == 1:
            xc[0].wait_recv()
            xc[1].wait_recv()
            yc[2].start()
            yc[3].start()

    has_up = y > 0
    has_down = y < S - 1
    yc[0].wait_recv()
    yc[1].wait_recv()
    zrow = jnp.zeros((COLS, CH), BF)

    def rims(f, _):
        PA[f, 0, :, 0:384] = shifted(jnp.where(has_up, YU[f], zrow))
        PA[f, 4, :, 384:768] = shifted(jnp.where(has_down, YD[f], zrow))
        return 0

    lax.fori_loop(2, 6, rims, 0)

    def rim_dots(lag, lo):
        n = FR - lo
        a = PA[lo + 2 - lag : FR + 2 - lag, 0].reshape(n * 256, 768)
        d = dot(a, W[lag, 0:768]).reshape(n, 256, 256)
        a2 = PA[lo + 2 - lag : FR + 2 - lag, 4].reshape(n * 256, 768)
        d2 = dot(a2, W[lag, 768:1536]).reshape(n, 256, 256)
        for i in range(lo, FR):
            acc[i, 0] += within[i][lag] * d[i - lo]
            acc[i, 3] += within[i][lag] * d2[i - lo]

    for lag in range(3):
        rim_dots(lag, lag)

    def stat(i, k):
        v = acc[i, k]
        s = jnp.sum(v, axis=0, keepdims=True)
        c = v - s * (1.0 / 256)
        q = jnp.sum(c * c, axis=0, keepdims=True)
        sS[i, pl.ds(k, 1)] = s
        sQ[i, pl.ds(k, 1)] = q

    def stat_loop(n, _):
        stat(2 + n // 4, n % 4)
        return 0

    lax.fori_loop(0, 8, stat_loop, 0)

    def early(p):
        a1 = PA[1, p]
        a2 = PA[0:2, p].reshape(512, 768)
        if p < 4:
            e = dot(a1, W[1, 0:768])
            g = dot(a2, W[2, 0:768])
            acc[0, p] += within[0][1] * e + within[0][2] * g[0:256]
            acc[1, p] += within[1][2] * g[256:512]
        if p > 0:
            e = dot(a1, W[1, 768:1536])
            g = dot(a2, W[2, 768:1536])
            acc[0, p - 1] += within[0][1] * e + within[0][2] * g[0:256]
            acc[1, p - 1] += within[1][2] * g[256:512]

    def early_rows(p):
        for f in range(2):
            PA[f, p, :, 0:384] = shifted(XH[f, 2 * p - 1])
            PA[f, p, :, 384:768] = shifted(XH[f, 2 * p])

    xc[2].wait_recv()
    early_rows(1)
    early(1)
    yc[2].wait_recv()
    yc[3].wait_recv()
    for f in range(2):
        PA[f, 0, :, 384:768] = shifted(XH[f, 0])
        PA[f, 4, :, 0:384] = shifted(XH[f, 7])
    lax.fori_loop(0, 2, rims, 0)
    early(0)
    early(4)
    stat(0, 0)
    stat(1, 0)
    xc[3].wait_recv()
    early_rows(2)
    early(2)
    stat(0, 1)
    stat(1, 1)
    xc[4].wait_recv()
    early_rows(3)
    early(3)
    stat(0, 2)
    stat(1, 2)
    stat(0, 3)
    stat(1, 3)

    means, squares = [], []
    for i in range(FR):
        s = sS[i]
        q = sQ[i]
        m = s * (1.0 / 256)
        tot = jnp.sum(s, axis=0, keepdims=True)
        mean = (tot[:, :128] + tot[:, 128:]) * (1.0 / 2048)
        both = jnp.concatenate([mean, mean], axis=1)
        dm = m - both
        qq = jnp.sum(q + 256.0 * dm * dm, axis=0, keepdims=True)
        means.append(mean)
        squares.append(qq[:, :128] + qq[:, 128:])
    mine = jnp.concatenate(means + squares, axis=0)
    st[...] = mine
    buf1[core * S + y] = mine

    s1 = []
    for i, (dc, dy) in enumerate(near):
        s1.append(rcopy(st, buf1.at[core * S + y], s1_s.at[i], s1_r.at[i], near_dev(dc, dy)))
    for c in s1:
        c.start()
    for c in s1:
        c.wait_recv()

    parts = []
    for c in range(2):
        b = buf1[pl.ds(c * S, S)]
        m = b[:, 0:4]
        mean = jnp.sum(m, axis=0) * (1.0 / S)
        dm = m - mean[None]
        parts.append((mean, jnp.sum(b[:, 4:8] + 2048.0 * dm * dm, axis=0)))
    chip_table = jnp.concatenate([parts[0][0], parts[1][0], parts[0][1], parts[1][1]], axis=0)
    ct[...] = chip_table
    buf2[2 * NX + cx] = chip_table

    s2 = []
    for i, (dz, dx) in enumerate(far):
        s2.append(rcopy(ct, buf2.at[(2 - dz) * NX + cx], s2_s.at[i], s2_r.at[i], far_dev(dz, dx)))
    for c in s2:
        c.start()
    for c in s2:
        c.wait_recv()

    shape = (5 * NX, 8, 128)
    slot = lax.broadcasted_iota(jnp.int32, shape, 0)
    row = lax.broadcasted_iota(jnp.int32, shape, 1)
    frame = ((cz - 2) * NX + slot) * 8 + row
    mean_e = buf2[:, 0:8]
    m2_e = buf2[:, 8:16]
    masks = [((frame >= starts[i]) & (frame < ends[i])).astype(F32) for i in range(FR)]
    lengths = [(ends[i] - starts[i]).astype(F32) for i in range(FR)]
    total = [jnp.sum(jnp.sum(masks[i] * mean_e, axis=0), axis=0, keepdims=True) / (lengths[i] * 4.0) for i in range(FR)]
    avg = group_sum(jnp.concatenate(total + total, axis=0))
    vs = []
    for i in range(FR):
        d = mean_e - avg[i : i + 1][None]
        e = masks[i] * (m2_e + 8192.0 * d * d)
        vs.append(jnp.sum(jnp.sum(e, axis=0), axis=0, keepdims=True) / (lengths[i] * (8192.0 * 4.0)))
    var = group_sum(jnp.concatenate(vs + vs, axis=0))
    rstd = lax.rsqrt(var + 1e-6)
    tab[...] = jnp.concatenate([avg[0:4], rstd[0:4]], axis=0)

    for c in xc + yc + s1 + s2:
        c.wait_send()


def norm_kernel(acc, tab, gain, shift, out):
    i = pl.program_id(0)
    avg = tab[pl.ds(i, 1)]
    scale = tab[pl.ds(i + 4, 1)] * gain[...]
    off = shift[...]
    for k in range(4):
        for h in range(2):
            v = (acc[0, k, :, h * 128 : (h + 1) * 128] - avg) * scale + off
            out[0, 2 * k + h] = (v * (1.0 / (1.0 + jnp.exp(-v)))).astype(BF)


def shards(frames, conv_weight, norm_gain, norm_shift, clip_lengths):
    V = pltpu.VMEM
    D = pltpu.SemaphoreType.DMA
    anyspec = pl.BlockSpec(memory_space=pltpu.HBM)
    vspec = pl.BlockSpec(memory_space=V)
    acc, tab = pl.pallas_call(
        conv_kernel,
        out_shape=(jax.ShapeDtypeStruct((FR, 4, 256, 256), F32), jax.ShapeDtypeStruct((8, 128), F32)),
        in_specs=[anyspec, anyspec, pl.BlockSpec(memory_space=pltpu.SMEM)],
        out_specs=(vspec, vspec),
        scratch_shapes=[
            V((4, 8, 256, 128), BF), V((2, 8, 256, 128), BF), V((6, 256, 128), BF), V((6, 256, 128), BF),
            V((6, 5, 256, 768), BF), V((3, 1536, 256), BF),
            V((4, 4, 256), F32), V((4, 4, 256), F32), V((8, 128), F32), V((16, 128), F32),
            V((8, 8, 128), F32), V((20, 16, 128), F32),
            D((4,)), D((6,)), D((5,)), D((5,)), D((4,)), D((4,)), D((7,)), D((7,)), D((19,)), D((19,)),
        ],
        compiler_params=pltpu.CompilerParams(collective_id=0, has_side_effects=True, vmem_limit_bytes=48 * 2**20),
        name="conv_stats",
    )(frames, conv_weight, clip_lengths)
    return pl.pallas_call(
        norm_kernel,
        grid=(FR,),
        out_shape=jax.ShapeDtypeStruct((FR, ROWS, COLS, CH), BF),
        in_specs=[
            pl.BlockSpec((1, 4, 256, 256), lambda i: (i, 0, 0, 0)),
            pl.BlockSpec((8, 128), lambda i: (0, 0)),
            pl.BlockSpec((1, 128), lambda i: (0, 0)),
            pl.BlockSpec((1, 128), lambda i: (0, 0)),
        ],
        out_specs=pl.BlockSpec((1, ROWS, COLS, CH), lambda i: (i, 0, 0, 0)),
        name="normalize",
    )(acc, tab, norm_gain.reshape(1, CH), norm_shift.reshape(1, CH))


def solution(mesh):
    return jax.shard_map(
        shards,
        mesh=mesh,
        in_specs=(P("tm", "space", None, None), P(), P(), P(), P()),
        out_specs=P("tm", "space", None, None),
        check_vma=False,
    )
```

time: 284 us -> 46.7 us (0.16)
  the two profiles are of different devices: /device:TPU:64 before, /device:TPU:1 now
where the time goes in v1:
time: 46.7 us; the launch traced here: 46.5 us
  Pallas kernels  42.5 us (91%)
  local copies, waits for them, and re-layouts  4 us (9%)
    pallas_call x1, Pallas kernels, shards(): pl.pallas_call(conv_kernel, out_shape=(jax.ShapeDtypeStruct((FR, 4, 256,...  37.7 us
    pallas_call x1, Pallas kernels, shards(): pl.pallas_call(norm_kernel, grid=(FR,), out_shape=jax.ShapeDtypeStruct((F...  4.79 us
    unnamed x8, local copies, waits for them, and re-layouts  4 us

profile of v1, /device:TPU:1, one launch (start us, length us, event | category | flops | bytes accessed | tf_op | source)
XLA Modules:
  0.0 46.5 jit_solution(9829553024723006610)
XLA Ops:
  0.0 0.0 copy-start
  0.0 1.6 %copy-done = bf16[4,8,256,128]{3,2,1,0:T(8,128)(2,1)S(1)} copy-done((bf16[4,8,256,128]{3,2,1,0:T(8,128)(2,1)S(1)}, bf16[4,8,256,128]{3,2,1,0:T(8,128)(2,1)}, u32[]{:S(2)}) %copy-start) | copy-done | bytes 2097176
  1.6 0.0 copy-start.1
  1.6 1.2 %copy-done.1 = bf16[3,1152,128]{2,1,0:T(8,128)(2,1)S(1)} copy-done((bf16[3,1152,128]{2,1,0:T(8,128)(2,1)S(1)}, bf16[3,1152,128]{2,1,0:T(8,128)(2,1)}, u32[]{:S(2)}) %copy-start.1) | copy-done | bytes 884760
  2.8 0.0 copy-start.3
  2.8 0.7 %copy-done.3 = s32[32]{0:T(128)S(1)} copy-done((s32[32]{0:T(128)S(1)}, s32[32]{0:T(128)}, u32[]{:S(2)}) %copy-start.3) | copy-done | bytes 152
  3.4 37.7 %conv_stats.1 = (f32[4,4,256,256]{3,2,1,0:T(8,128)}, f32[8,128]{1,0:T(8,128)S(1)}) custom-call(bf16[4,8,256,128]{3,2,1,0:T(8,128)(2,1)S(1)} %copy-done, bf16[3,1152,128]{2,1,0:T(8,128)(2,1)S(1)} %copy-done.1, s32[32]{0:T(128)S(1)} %copy-done.3), custom_call_target="tpu_custom_call" | custom-call | tf_op jit(solution)/shard_map/conv_stats/pallas_call | solution.py:324
  41.1 0.0 copy-start.2
  41.1 0.6 %copy-done.2 = f32[8,128]{1,0:T(8,128)} copy-done((f32[8,128]{1,0:T(8,128)}, f32[8,128]{1,0:T(8,128)S(1)}, u32[]{:S(2)}) %copy-start.2) | copy-done | bytes 4120
  41.7 4.8 %normalize.1 = bf16[4,8,256,128]{3,2,1,0:T(8,128)(2,1)} custom-call(f32[4,4,256,256]{3,2,1,0:T(8,128)} %get-tuple-element.7.acc, f32[8,128]{1,0:T(8,128)} %copy-done.2, f32[1,128]{1,0:T(1,128)} %bitcast.2, f32[1,128]{1,0:T(1,128)} %bitcast.3), custom_call_target="tpu_custom_call" | custom-call | tf_op jit(solution)/shard_map/normalize/pallas_call | solution.py:339
Async XLA Ops:
  0.0 1.6 %copy-start = (bf16[4,8,256,128]{3,2,1,0:T(8,128)(2,1)S(1)}, bf16[4,8,256,128]{3,2,1,0:T(8,128)(2,1)}, u32[]{:S(2)}) copy-start(bf16[4,8,256,128]{3,2,1,0:T(8,128)(2,1)} %x.1) | copy-start | bytes 6291460
  1.6 1.2 %copy-start.1 = (bf16[3,1152,128]{2,1,0:T(8,128)(2,1)S(1)}, bf16[3,1152,128]{2,1,0:T(8,128)(2,1)}, u32[]{:S(2)}) copy-start(bf16[3,1152,128]{2,1,0:T(8,128)(2,1)} %w.1) | copy-start | bytes 2654212
  2.8 0.7 %copy-start.3 = (s32[32]{0:T(128)S(1)}, s32[32]{0:T(128)}, u32[]{:S(2)}) copy-start(s32[32]{0:T(128)} %lens.1) | copy-start | bytes 388
  41.1 0.6 %copy-start.2 = (f32[8,128]{1,0:T(8,128)}, f32[8,128]{1,0:T(8,128)S(1)}, u32[]{:S(2)}) copy-start(f32[8,128]{1,0:T(8,128)S(1)} %get-tuple-element.8.tab) | copy-start | bytes 12292

commit v2 on v1

--- a/solution.py
+++ b/solution.py
@@ -28,8 +28,8 @@
     return x + jnp.where(lane % 4 < 2, pltpu.roll(x, n - 2, 1), pltpu.roll(x, 2, 1))
 
 
-def conv_kernel(x, w, lens, acc, tab, XL, XH, YU, YD, PA, W, sS, sQ, st, ct, buf1, buf2,
-                lsem, wsem, xsem_s, xsem_r, ysem_s, ysem_r, s1_s, s1_r, s2_s, s2_r):
+def conv_kernel(x, w, lens_hbm, acc, tab, lens, XL, XH, YU, YD, PA, W, sS, sQ, st, ct, buf1, buf2,
+                lensem, tok, tok2, lsem, wsem, xsem_s, xsem_r, ysem_s, ysem_r, s1_s, s1_r, s2_s, s2_r):
     t = lax.axis_index("tm")
     y = lax.axis_index("space")
     core = t % 2
@@ -44,14 +44,8 @@
     up = (t, (y + 1) % S)
     down = (t, (y + S - 1) % S)
 
-    near = [(dc, dy) for dc in range(2) for dy in range(S) if (dc, dy) != (0, 0)]
+    near = [(dc, dy) for dc in range(2) for dy in (2, 1, 3, 0) if (dc, dy) != (0, 0)]
     far = [(dz, dx) for dz in (2, -2, 1, -1, 0) for dx in (2, 1, 3, 0) if (dz, dx) != (0, 0)]
-    barrier = pltpu.get_barrier_semaphore()
-
-    def greet(d):
-        pl.semaphore_signal(barrier, inc=1, device_id=d, device_id_type=MESH)
-
-    greet(((t + 2 * core - 1 + T) % T, y))
 
     def near_dev(dc, dy):
         return dev(cz, cx, (core + dc) % 2, (y + dy) % S)
@@ -59,11 +53,18 @@
     def far_dev(dz, dx):
         return dev((cz + dz + NZ) % NZ, (cx + dx) % NX, core, y)
 
-    for dc, dy in near:
-        greet(near_dev(dc, dy))
-    for dz, dx in far:
-        greet(far_dev(dz, dx))
-
+    prev = ((t + T - 1) % T, y)
+    direct = [nxt, up, down, prev, far_dev(0, 1), far_dev(0, 3), far_dev(1, 0), far_dev(-1, 0)]
+    second = [far_dev(2, 0), far_dev(-2, 0), far_dev(1, 0), far_dev(-1, 0), near_dev(1, 0)]
+    barrier = pltpu.get_barrier_semaphore()
+
+    def greet(sem, devices):
+        for d in devices:
+            pl.semaphore_signal(sem, inc=1, device_id=d, device_id_type=MESH)
+
+    greet(barrier, direct)
+    lens_load = pltpu.make_async_copy(lens_hbm, lens, lensem)
+    lens_load.start()
     loads = [pltpu.make_async_copy(x.at[f], XL.at[f], lsem.at[f]) for f in range(FR)]
     wloads = []
     for lag in range(3):
@@ -72,7 +73,11 @@
     for c in loads + wloads:
         c.start()
 
-    pl.semaphore_wait(barrier, 1 + len(near) + len(far))
+    for lag in range(3):
+        W[lag, 1152:1536, 0:128] = jnp.zeros((384, 128), BF)
+        W[lag, 0:384, 128:256] = jnp.zeros((384, 128), BF)
+
+    pl.semaphore_wait(barrier, len(direct))
 
     def rcopy(src, dst, ss, rs, d):
         return pltpu.make_async_remote_copy(src_ref=src, dst_ref=dst, send_sem=ss, recv_sem=rs, device_id=d, device_id_type=MESH)
@@ -93,7 +98,9 @@
     xc[2].start()
     xc[3].start()
     xc[4].start()
-
+    greet(tok, direct)
+
+    lens_load.wait()
     pos = [t * FR + i for i in range(FR)]
 
     def bounds(k, c):
@@ -108,47 +115,39 @@
     _, starts, ends = lax.fori_loop(0, 32, bounds, (zero, (zero,) * FR, (zero,) * FR))
     within = [[jnp.where(pos[i] - lag >= starts[i], 1.0, 0.0).astype(F32) for lag in range(3)] for i in range(FR)]
 
-    for lag in range(3):
-        W[lag, 1152:1536, 0:128] = jnp.zeros((384, 128), BF)
-        W[lag, 0:384, 128:256] = jnp.zeros((384, 128), BF)
-
-    for f in range(FR):
-        loads[f].wait()
-
-        def pairs(p, _, f=f):
-            PA[f + 2, p, :, 0:384] = shifted(XL[f, 2 * p - 1])
-            PA[f + 2, p, :, 384:768] = shifted(XL[f, 2 * p])
-            return 0
-
-        lax.fori_loop(1, 4, pairs, 0)
-        PA[f + 2, 0, :, 384:768] = shifted(XL[f, 0])
-        PA[f + 2, 4, :, 0:384] = shifted(XL[f, 7])
-    for c in wloads:
-        c.wait()
+    def build(f):
+        for r in range(ROWS):
+            e = r + 1
+            PA[f + 2, e // 2, :, (e % 2) * 384 : (e % 2 + 1) * 384] = shifted(XL[f, r])
 
     def dot(a, b):
         return jnp.dot(a, b, preferred_element_type=F32)
 
-    def local(i, lag):
+    def unit(i, lag, first):
         a = PA[i + 2 - lag, 1:4].reshape(768, 768)
         d1 = dot(a, W[lag, 768:1536]).reshape(3, 256, 256)
         d0 = dot(a, W[lag, 0:768]).reshape(3, 256, 256)
-        return d1, d0
-
-    for i in range(FR):
-        d1, d0 = local(i, 0)
-        acc[i, 0] = d1[0]
-        acc[i, 1] = d1[1] + d0[0]
-        acc[i, 2] = d1[2] + d0[1]
-        acc[i, 3] = d0[2]
-        for lag in range(1, min(i, 2) + 1):
-            d1, d0 = local(i, lag)
-            s = within[i][lag]
-            acc[i, 0] += s * d1[0]
-            acc[i, 1] += s * (d1[1] + d0[0])
-            acc[i, 2] += s * (d1[2] + d0[1])
-            acc[i, 3] += s * d0[2]
-        if i == 1:
+        parts = [d1[0], d1[1] + d0[0], d1[2] + d0[1], d0[2]]
+        for k in range(4):
+            v = parts[k] if lag == 0 else within[i][lag] * parts[k]
+            if first:
+                acc[i, k] = v
+            else:
+                acc[i, k] += v
+
+    for c in loads:
+        c.wait()
+    for c in wloads:
+        c.wait()
+    build(0)
+    for f in range(FR):
+        for lag in range(min(2, FR - 1 - f), -1, -1):
+            unit(f + lag, lag, lag == min(2, f + lag))
+        if f + 1 < FR:
+            build(f + 1)
+        if f == 1:
+            pl.semaphore_wait(tok, len(direct))
+            greet(tok2, second)
             xc[0].wait_recv()
             xc[1].wait_recv()
             yc[2].start()
@@ -258,8 +257,11 @@
     s1 = []
     for i, (dc, dy) in enumerate(near):
         s1.append(rcopy(st, buf1.at[core * S + y], s1_s.at[i], s1_r.at[i], near_dev(dc, dy)))
+    pl.semaphore_wait(tok2, len(second))
     for c in s1:
         c.start()
+    for c in xc + yc:
+        c.wait_send()
     for c in s1:
         c.wait_recv()
 
@@ -279,6 +281,9 @@
         s2.append(rcopy(ct, buf2.at[(2 - dz) * NX + cx], s2_s.at[i], s2_r.at[i], far_dev(dz, dx)))
     for c in s2:
         c.start()
+    for c in s1:
+        c.wait_send()
+    weight = [1.0 / (jnp.full((1, 128), 4.0, F32) * (ends[i] - starts[i]).astype(F32)) for i in range(FR)]
     for c in s2:
         c.wait_recv()
 
@@ -289,66 +294,78 @@
     mean_e = buf2[:, 0:8]
     m2_e = buf2[:, 8:16]
     masks = [((frame >= starts[i]) & (frame < ends[i])).astype(F32) for i in range(FR)]
-    lengths = [(ends[i] - starts[i]).astype(F32) for i in range(FR)]
-    total = [jnp.sum(jnp.sum(masks[i] * mean_e, axis=0), axis=0, keepdims=True) / (lengths[i] * 4.0) for i in range(FR)]
+    total = [jnp.sum(jnp.sum(masks[i] * mean_e, axis=0), axis=0, keepdims=True) * weight[i] for i in range(FR)]
     avg = group_sum(jnp.concatenate(total + total, axis=0))
     vs = []
     for i in range(FR):
         d = mean_e - avg[i : i + 1][None]
         e = masks[i] * (m2_e + 8192.0 * d * d)
-        vs.append(jnp.sum(jnp.sum(e, axis=0), axis=0, keepdims=True) / (lengths[i] * (8192.0 * 4.0)))
+        vs.append(jnp.sum(jnp.sum(e, axis=0), axis=0, keepdims=True) * (weight[i] * (1.0 / 8192)))
     var = group_sum(jnp.concatenate(vs + vs, axis=0))
     rstd = lax.rsqrt(var + 1e-6)
     tab[...] = jnp.concatenate([avg[0:4], rstd[0:4]], axis=0)
 
-    for c in xc + yc + s1 + s2:
+    for c in s2:
         c.wait_send()
 
 
-def norm_kernel(acc, tab, gain, shift, out):
-    i = pl.program_id(0)
-    avg = tab[pl.ds(i, 1)]
-    scale = tab[pl.ds(i + 4, 1)] * gain[...]
-    off = shift[...]
-    for k in range(4):
-        for h in range(2):
-            v = (acc[0, k, :, h * 128 : (h + 1) * 128] - avg) * scale + off
-            out[0, 2 * k + h] = (v * (1.0 / (1.0 + jnp.exp(-v)))).astype(BF)
+def norm_kernel(acc, tab, gain, shift, out, buf, sem):
+    off = shift[...] * 0.5
+    copies = []
+    for c in range(8):
+        i, p = c // 2, 2 * (c % 2)
+        avg = tab[i : i + 1]
+        scale = tab[i + 4 : i + 5] * gain[...] * 0.5
+        for k in (p, p + 1):
+            for h in range(2):
+                v = (acc[i, k, :, h * 128 : (h + 1) * 128] - avg) * scale + off
+                buf[i, 2 * k + h] = (v + v * jnp.tanh(v)).astype(BF)
+        copies.append(pltpu.make_async_copy(buf.at[i, pl.ds(2 * p, 4)], out.at[i, pl.ds(2 * p, 4)], sem.at[c]))
+        copies[-1].start()
+    for c in copies:
+        c.wait()
 
 
 def shards(frames, conv_weight, norm_gain, norm_shift, clip_lengths):
     V = pltpu.VMEM
+
+    def hbm(a):
+        return pltpu.with_memory_space_constraint(a, pltpu.HBM)
+
     D = pltpu.SemaphoreType.DMA
     anyspec = pl.BlockSpec(memory_space=pltpu.HBM)
     vspec = pl.BlockSpec(memory_space=V)
     acc, tab = pl.pallas_call(
         conv_kernel,
-        out_shape=(jax.ShapeDtypeStruct((FR, 4, 256, 256), F32), jax.ShapeDtypeStruct((8, 128), F32)),
-        in_specs=[anyspec, anyspec, pl.BlockSpec(memory_space=pltpu.SMEM)],
+        out_shape=(pltpu.VMEM((FR, 4, 256, 256), F32), pltpu.VMEM((8, 128), F32)),
+        in_specs=[anyspec, anyspec, anyspec],
         out_specs=(vspec, vspec),
         scratch_shapes=[
+            pltpu.SMEM((32,), jnp.int32),
             V((4, 8, 256, 128), BF), V((2, 8, 256, 128), BF), V((6, 256, 128), BF), V((6, 256, 128), BF),
             V((6, 5, 256, 768), BF), V((3, 1536, 256), BF),
             V((4, 4, 256), F32), V((4, 4, 256), F32), V((8, 128), F32), V((16, 128), F32),
             V((8, 8, 128), F32), V((20, 16, 128), F32),
+            D, pltpu.SemaphoreType.REGULAR, pltpu.SemaphoreType.REGULAR,
             D((4,)), D((6,)), D((5,)), D((5,)), D((4,)), D((4,)), D((7,)), D((7,)), D((19,)), D((19,)),
         ],
-        compiler_params=pltpu.CompilerParams(collective_id=0, has_side_effects=True, vmem_limit_bytes=48 * 2**20),
+        compiler_params=pltpu.CompilerParams(collective_id=0, has_side_effects=True, vmem_limit_bytes=56 * 2**20),
         name="conv_stats",
-    )(frames, conv_weight, clip_lengths)
+    )(hbm(frames), hbm(conv_weight), hbm(clip_lengths))
     return pl.pallas_call(
         norm_kernel,
-        grid=(FR,),
         out_shape=jax.ShapeDtypeStruct((FR, ROWS, COLS, CH), BF),
-        in_specs=[
-            pl.BlockSpec((1, 4, 256, 256), lambda i: (i, 0, 0, 0)),
-            pl.BlockSpec((8, 128), lambda i: (0, 0)),
-            pl.BlockSpec((1, 128), lambda i: (0, 0)),
-            pl.BlockSpec((1, 128), lambda i: (0, 0)),
-        ],
-        out_specs=pl.BlockSpec((1, ROWS, COLS, CH), lambda i: (i, 0, 0, 0)),
+        in_specs=[vspec, vspec, vspec, vspec],
+        out_specs=anyspec,
+        scratch_shapes=[V((FR, ROWS, COLS, CH), BF), D((8,))],
+        compiler_params=pltpu.CompilerParams(vmem_limit_bytes=8 * 2**20),
         name="normalize",
-    )(acc, tab, norm_gain.reshape(1, CH), norm_shift.reshape(1, CH))
+    )(
+        pltpu.with_memory_space_constraint(acc, V),
+        pltpu.with_memory_space_constraint(tab, V),
+        norm_gain.reshape(1, CH),
+        norm_shift.reshape(1, CH),
+    )
 
 
 def solution(mesh):

time: 46.7 us -> 36.4 us (0.78)
  Pallas kernels: 42.5 us -> 36.1 us
  local copies, waits for them, and re-layouts: 4 us -> 0.01 us
    pallas_call x2, Pallas kernels: 42.5 us -> 36.1 us  [the longest x1 34.5 us: shards(): pl.pallas_call(conv_kernel, out_shape=(pltpu.VMEM((FR, 4, 256, 256), F32)...]
    unnamed x8 -> x4, local copies, waits for them, and re-layouts: 4 us -> 0.01 us
where the time goes in v2:
time: 36.4 us; the launch traced here: 36.3 us
  Pallas kernels  36.1 us (99%)
    pallas_call x1, Pallas kernels, shards(): pl.pallas_call(conv_kernel, out_shape=(pltpu.VMEM((FR, 4, 256, 256), F32)...  34.5 us
    pallas_call x1, Pallas kernels, shards(): pl.pallas_call(norm_kernel, out_shape=jax.ShapeDtypeStruct((FR, ROWS, COL...  1.67 us

profile of v2, /device:TPU:1, one launch (start us, length us, event | category | flops | bytes accessed | tf_op | source)
XLA Modules:
  0.0 36.3 jit_solution(6732917987238709133)
XLA Ops:
  0.0 0.0 copy-start.1
  0.0 0.0 copy-start
  0.0 34.5 %conv_stats.1 = (f32[4,4,256,256]{3,2,1,0:T(8,128)S(1)}, f32[8,128]{1,0:T(8,128)S(1)}) custom-call(bf16[4,8,256,128]{3,2,1,0:T(8,128)(2,1)} %x.1, bf16[3,1152,128]{2,1,0:T(8,128)(2,1)} %w.1, s32[32]{0:T(128)} %lens_hbm.1), custom_call_target="tpu_custom_call" | custom-call | tf_op jit(solution)/shard_map/conv_stats/pallas_call | solution.py:338
  34.5 0.0 copy-done.1
  34.5 0.0 copy-done
  34.5 1.7 %normalize.1 = bf16[4,8,256,128]{3,2,1,0:T(8,128)(2,1)} custom-call(f32[4,4,256,256]{3,2,1,0:T(8,128)S(1)} %get-tuple-element.7.acc, f32[8,128]{1,0:T(8,128)S(1)} %get-tuple-element.8.tab, f32[1,128]{1,0:T(1,128)S(1)} %bitcast.2, f32[1,128]{1,0:T(1,128)S(1)} %bitcast.3), custom_call_target="tpu_custom_call" | custom-call | tf_op jit(solution)/shard_map/normalize/pallas_call | solution.py:355
Async XLA Ops:
  0.0 34.5 %copy-start.1 = (f32[128]{0:T(128)S(1)}, f32[128]{0:T(128)}, u32[]{:S(2)}) copy-start(f32[128]{0:T(128)} %param.8) | copy-start | bytes 1540
  0.0 34.5 %copy-start = (f32[128]{0:T(128)S(1)}, f32[128]{0:T(128)}, u32[]{:S(2)}) copy-start(f32[128]{0:T(128)} %param.7) | copy-start | bytes 1540

commit v3 on v2

--- a/solution.py
+++ b/solution.py
@@ -53,31 +53,45 @@
     def far_dev(dz, dx):
         return dev((cz + dz + NZ) % NZ, (cx + dx) % NX, core, y)
 
+    has_next = t < T - 1
+    has_prev = t > 0
+
+    def has_z(dz):
+        return (cz + dz >= 0) & (cz + dz < NZ)
+
     prev = ((t + T - 1) % T, y)
-    direct = [nxt, up, down, prev, far_dev(0, 1), far_dev(0, 3), far_dev(1, 0), far_dev(-1, 0)]
-    second = [far_dev(2, 0), far_dev(-2, 0), far_dev(1, 0), far_dev(-1, 0), near_dev(1, 0)]
+    direct = [(nxt, has_next), (up, None), (down, None), (prev, has_prev), (far_dev(0, 1), None), (far_dev(0, 3), None),
+              (far_dev(1, 0), has_z(1)), (far_dev(-1, 0), has_z(-1))]
+    second = [(far_dev(2, 0), has_z(2)), (far_dev(-2, 0), has_z(-2)), (far_dev(1, 0), has_z(1)), (far_dev(-1, 0), has_z(-1)),
+              (near_dev(1, 0), None)]
     barrier = pltpu.get_barrier_semaphore()
 
     def greet(sem, devices):
-        for d in devices:
-            pl.semaphore_signal(sem, inc=1, device_id=d, device_id_type=MESH)
-
+        for d, cond in devices:
+            def signal(d=d):
+                pl.semaphore_signal(sem, inc=1, device_id=d, device_id_type=MESH)
+            if cond is None:
+                signal()
+            else:
+                pl.when(cond)(signal)
+
+    def count(devices):
+        return sum(jnp.int32(1) if cond is None else cond.astype(jnp.int32) for _, cond in devices)
+
+    buf2[...] = jnp.zeros_like(buf2)
     greet(barrier, direct)
     lens_load = pltpu.make_async_copy(lens_hbm, lens, lensem)
     lens_load.start()
     loads = [pltpu.make_async_copy(x.at[f], XL.at[f], lsem.at[f]) for f in range(FR)]
-    wloads = []
-    for lag in range(3):
-        wloads.append(pltpu.make_async_copy(w.at[lag], W.at[lag, pl.ds(0, 1152), pl.ds(0, 128)], wsem.at[lag]))
-        wloads.append(pltpu.make_async_copy(w.at[lag], W.at[lag, pl.ds(384, 1152), pl.ds(128, 128)], wsem.at[3 + lag]))
-    for c in loads + wloads:
+    wloads = [pltpu.make_async_copy(w.at[lag], W.at[lag, pl.ds(0, 1152), pl.ds(0, 128)], wsem.at[lag]) for lag in range(3)]
+    for c in [loads[0]] + wloads + loads[1:]:
         c.start()
 
     for lag in range(3):
         W[lag, 1152:1536, 0:128] = jnp.zeros((384, 128), BF)
         W[lag, 0:384, 128:256] = jnp.zeros((384, 128), BF)
 
-    pl.semaphore_wait(barrier, len(direct))
+    pl.semaphore_wait(barrier, count(direct))
 
     def rcopy(src, dst, ss, rs, d):
         return pltpu.make_async_remote_copy(src_ref=src, dst_ref=dst, send_sem=ss, recv_sem=rs, device_id=d, device_id_type=MESH)
@@ -91,13 +105,29 @@
         rcopy(XH.at[:, 7], YU.at[pl.ds(0, 2)], ysem_s.at[2], ysem_r.at[2], up),
         rcopy(XH.at[:, 0], YD.at[pl.ds(0, 2)], ysem_s.at[3], ysem_r.at[3], down),
     ]
-    xc[0].start()
-    xc[1].start()
+    @pl.when(has_next)
+    def _():
+        xc[0].start()
+        xc[1].start()
+
     yc[0].start()
     yc[1].start()
-    xc[2].start()
-    xc[3].start()
-    xc[4].start()
+
+    @pl.when(has_next)
+    def _():
+        for c in xc[2:]:
+            c.start()
+
+    @pl.when(jnp.logical_not(has_prev))
+    def _():
+        XH[...] = jnp.zeros_like(XH)
+
+    def landed(*copies):
+        @pl.when(has_prev)
+        def _():
+            for c in copies:
+                c.wait_recv()
+
     greet(tok, direct)
 
     lens_load.wait()
@@ -123,35 +153,43 @@
     def dot(a, b):
         return jnp.dot(a, b, preferred_element_type=F32)
 
-    def unit(i, lag, first):
-        a = PA[i + 2 - lag, 1:4].reshape(768, 768)
-        d1 = dot(a, W[lag, 768:1536]).reshape(3, 256, 256)
-        d0 = dot(a, W[lag, 0:768]).reshape(3, 256, 256)
-        parts = [d1[0], d1[1] + d0[0], d1[2] + d0[1], d0[2]]
-        for k in range(4):
-            v = parts[k] if lag == 0 else within[i][lag] * parts[k]
-            if first:
-                acc[i, k] = v
-            else:
-                acc[i, k] += v
-
     for c in loads:
         c.wait()
-    for c in wloads:
-        c.wait()
     build(0)
+    for lag in range(3):
+        wloads[lag].wait()
+        W[lag, 384:1536, 128:256] = W[lag, 0:1152, 0:128]
     for f in range(FR):
-        for lag in range(min(2, FR - 1 - f), -1, -1):
-            unit(f + lag, lag, lag == min(2, f + lag))
+        tot = None
+        for lag in range(min(f, 2), -1, -1):
+            a = PA[f + 2 - lag, 1:4].reshape(768, 768)
+            d1 = dot(a, W[lag, 768:1536])
+            d0 = dot(a, W[lag, 0:768])
+            if lag:
+                d1 = d1 * within[f][lag]
+                d0 = d0 * within[f][lag]
+            tot = (d1, d0) if tot is None else (tot[0] + d1, tot[1] + d0)
+        d1, d0 = tot[0].reshape(3, 256, 256), tot[1].reshape(3, 256, 256)
+        acc[f, 0] = d1[0]
+        acc[f, 1] = d1[1] + d0[0]
+        acc[f, 2] = d1[2] + d0[1]
+        acc[f, 3] = d0[2]
         if f + 1 < FR:
             build(f + 1)
         if f == 1:
-            pl.semaphore_wait(tok, len(direct))
+            pl.semaphore_wait(tok, count(direct))
             greet(tok2, second)
-            xc[0].wait_recv()
-            xc[1].wait_recv()
+            landed(xc[0], xc[1])
             yc[2].start()
             yc[3].start()
+
+    def stat(i, k):
+        v = acc[i, k]
+        s = jnp.sum(v, axis=0, keepdims=True)
+        c = v - s * (1.0 / 256)
+        q = jnp.sum(c * c, axis=0, keepdims=True)
+        sS[i, k : k + 1] = s
+        sQ[i, k : k + 1] = q
 
     has_up = y > 0
     has_down = y < S - 1
@@ -164,7 +202,8 @@
         PA[f, 4, :, 384:768] = shifted(jnp.where(has_down, YD[f], zrow))
         return 0
 
-    lax.fori_loop(2, 6, rims, 0)
+    for f in range(2, 6):
+        rims(f, 0)
 
     def rim_dots(lag, lo):
         n = FR - lo
@@ -178,20 +217,8 @@
 
     for lag in range(3):
         rim_dots(lag, lag)
-
-    def stat(i, k):
-        v = acc[i, k]
-        s = jnp.sum(v, axis=0, keepdims=True)
-        c = v - s * (1.0 / 256)
-        q = jnp.sum(c * c, axis=0, keepdims=True)
-        sS[i, pl.ds(k, 1)] = s
-        sQ[i, pl.ds(k, 1)] = q
-
-    def stat_loop(n, _):
-        stat(2 + n // 4, n % 4)
-        return 0
-
-    lax.fori_loop(0, 8, stat_loop, 0)
+    for i, k in ((2, 1), (2, 2), (3, 1), (3, 2)):
+        stat(i, k)
 
     def early(p):
         a1 = PA[1, p]
@@ -212,101 +239,115 @@
             PA[f, p, :, 0:384] = shifted(XH[f, 2 * p - 1])
             PA[f, p, :, 384:768] = shifted(XH[f, 2 * p])
 
-    xc[2].wait_recv()
+    landed(xc[2])
     early_rows(1)
     early(1)
+    for i, k in ((2, 0), (2, 3), (3, 0), (3, 3)):
+        stat(i, k)
     yc[2].wait_recv()
     yc[3].wait_recv()
     for f in range(2):
         PA[f, 0, :, 384:768] = shifted(XH[f, 0])
         PA[f, 4, :, 0:384] = shifted(XH[f, 7])
-    lax.fori_loop(0, 2, rims, 0)
+    for f in range(2):
+        rims(f, 0)
     early(0)
     early(4)
+    landed(xc[3])
+    early_rows(2)
+    early(2)
     stat(0, 0)
     stat(1, 0)
-    xc[3].wait_recv()
-    early_rows(2)
-    early(2)
-    stat(0, 1)
-    stat(1, 1)
-    xc[4].wait_recv()
+    landed(xc[4])
     early_rows(3)
     early(3)
-    stat(0, 2)
-    stat(1, 2)
-    stat(0, 3)
-    stat(1, 3)
-
+    for i, k in ((0, 1), (1, 1), (0, 2), (1, 2), (0, 3), (1, 3)):
+        stat(i, k)
+
+    lane = lax.broadcasted_iota(jnp.int32, (FR, 128), 1) % 4
     means, squares = [], []
     for i in range(FR):
         s = sS[i]
-        q = sQ[i]
         m = s * (1.0 / 256)
         tot = jnp.sum(s, axis=0, keepdims=True)
         mean = (tot[:, :128] + tot[:, 128:]) * (1.0 / 2048)
-        both = jnp.concatenate([mean, mean], axis=1)
-        dm = m - both
-        qq = jnp.sum(q + 256.0 * dm * dm, axis=0, keepdims=True)
+        dm = m - jnp.concatenate([mean, mean], axis=1)
+        qq = jnp.sum(sQ[i] + 256.0 * dm * dm, axis=0, keepdims=True)
         means.append(mean)
         squares.append(qq[:, :128] + qq[:, 128:])
-    mine = jnp.concatenate(means + squares, axis=0)
+    m = jnp.concatenate(means, axis=0)
+    g = group_sum(m) * 0.25
+    dm = m - g
+    mine = jnp.where(lane == 0, g, group_sum(jnp.concatenate(squares, axis=0) + 2048.0 * dm * dm))
     st[...] = mine
     buf1[core * S + y] = mine
 
     s1 = []
     for i, (dc, dy) in enumerate(near):
         s1.append(rcopy(st, buf1.at[core * S + y], s1_s.at[i], s1_r.at[i], near_dev(dc, dy)))
-    pl.semaphore_wait(tok2, len(second))
+    pl.semaphore_wait(tok2, count(second))
     for c in s1:
         c.start()
-    for c in xc + yc:
+
+    @pl.when(has_next)
+    def _():
+        for c in xc:
+            c.wait_send()
+
+    for c in yc:
         c.wait_send()
+    weight = [1.0 / (jnp.full((1, 128), 1.0, F32) * (ends[i] - starts[i]).astype(F32)) for i in range(FR)]
     for c in s1:
         c.wait_recv()
 
     parts = []
     for c in range(2):
         b = buf1[pl.ds(c * S, S)]
-        m = b[:, 0:4]
-        mean = jnp.sum(m, axis=0) * (1.0 / S)
-        dm = m - mean[None]
-        parts.append((mean, jnp.sum(b[:, 4:8] + 2048.0 * dm * dm, axis=0)))
-    chip_table = jnp.concatenate([parts[0][0], parts[1][0], parts[0][1], parts[1][1]], axis=0)
+        tot = jnp.sum(b, axis=0)
+        mean = tot * (1.0 / S)
+        dm = b - mean[None]
+        parts.append(jnp.where(lane == 0, mean, tot + 8192.0 * pltpu.roll(jnp.sum(dm * dm, axis=0), 1, 1)))
+    chip_table = jnp.concatenate(parts, axis=0)
     ct[...] = chip_table
     buf2[2 * NX + cx] = chip_table
 
-    s2 = []
+    s2 = {}
     for i, (dz, dx) in enumerate(far):
-        s2.append(rcopy(ct, buf2.at[(2 - dz) * NX + cx], s2_s.at[i], s2_r.at[i], far_dev(dz, dx)))
-    for c in s2:
-        c.start()
+        c = rcopy(ct, buf2.at[(2 - dz) * NX + cx], s2_s.at[i], s2_r.at[i], far_dev(dz, dx))
+        s2.setdefault(dz, []).append(c)
+
+    def each(dz, there, act):
+        def run():
+            for c in s2[dz]:
+                act(c)
+        pl.when(has_z(there))(run)
+
+    for dz in s2:
+        each(dz, dz, lambda c: c.start())
     for c in s1:
         c.wait_send()
-    weight = [1.0 / (jnp.full((1, 128), 4.0, F32) * (ends[i] - starts[i]).astype(F32)) for i in range(FR)]
-    for c in s2:
-        c.wait_recv()
+    for dz in s2:
+        each(dz, -dz, lambda c: c.wait_recv())
 
     shape = (5 * NX, 8, 128)
-    slot = lax.broadcasted_iota(jnp.int32, shape, 0)
-    row = lax.broadcasted_iota(jnp.int32, shape, 1)
-    frame = ((cz - 2) * NX + slot) * 8 + row
-    mean_e = buf2[:, 0:8]
-    m2_e = buf2[:, 8:16]
-    masks = [((frame >= starts[i]) & (frame < ends[i])).astype(F32) for i in range(FR)]
-    total = [jnp.sum(jnp.sum(masks[i] * mean_e, axis=0), axis=0, keepdims=True) * weight[i] for i in range(FR)]
-    avg = group_sum(jnp.concatenate(total + total, axis=0))
-    vs = []
+    frame = ((cz - 2) * NX + lax.broadcasted_iota(jnp.int32, shape, 0)) * 8 + lax.broadcasted_iota(jnp.int32, shape, 1)
+    entry = buf2[...]
+    avgs, vs = [], []
     for i in range(FR):
-        d = mean_e - avg[i : i + 1][None]
-        e = masks[i] * (m2_e + 8192.0 * d * d)
-        vs.append(jnp.sum(jnp.sum(e, axis=0), axis=0, keepdims=True) * (weight[i] * (1.0 / 8192)))
-    var = group_sum(jnp.concatenate(vs + vs, axis=0))
-    rstd = lax.rsqrt(var + 1e-6)
-    tab[...] = jnp.concatenate([avg[0:4], rstd[0:4]], axis=0)
-
-    for c in s2:
-        c.wait_send()
+        mask = ((frame >= starts[i]) & (frame < ends[i])).astype(F32)
+        tot = jnp.sum(jnp.sum(mask * entry, axis=0), axis=0, keepdims=True) * weight[i]
+        d = entry - tot[None]
+        dd = jnp.sum(jnp.sum(mask * (d * d), axis=0), axis=0, keepdims=True) * weight[i]
+        avgs.append(tot)
+        vs.append(tot * (1.0 / 32768) + pltpu.roll(dd, 1, 1))
+    both = jnp.concatenate(avgs + vs, axis=0)
+    lane8 = lax.broadcasted_iota(jnp.int32, (8, 128), 1) % 4
+    row8 = lax.broadcasted_iota(jnp.int32, (8, 128), 0)
+    both = group_sum(jnp.where(lane8 == jnp.where(row8 < 4, 0, 1), both, 0.0))
+    tab[...] = jnp.where(row8 < 4, both, lax.rsqrt(both + 1e-6))
+
+    for dz in s2:
+        each(dz, dz, lambda c: c.wait_send())
 
 
 def norm_kernel(acc, tab, gain, shift, out, buf, sem):
@@ -344,10 +385,10 @@
             pltpu.SMEM((32,), jnp.int32),
             V((4, 8, 256, 128), BF), V((2, 8, 256, 128), BF), V((6, 256, 128), BF), V((6, 256, 128), BF),
             V((6, 5, 256, 768), BF), V((3, 1536, 256), BF),
-            V((4, 4, 256), F32), V((4, 4, 256), F32), V((8, 128), F32), V((16, 128), F32),
-            V((8, 8, 128), F32), V((20, 16, 128), F32),
+            V((4, 4, 256), F32), V((4, 4, 256), F32), V((4, 128), F32), V((8, 128), F32),
+            V((8, 4, 128), F32), V((20, 8, 128), F32),
             D, pltpu.SemaphoreType.REGULAR, pltpu.SemaphoreType.REGULAR,
-            D((4,)), D((6,)), D((5,)), D((5,)), D((4,)), D((4,)), D((7,)), D((7,)), D((19,)), D((19,)),
+            D((4,)), D((3,)), D((5,)), D((5,)), D((4,)), D((4,)), D((7,)), D((7,)), D((19,)), D((19,)),
         ],
         compiler_params=pltpu.CompilerParams(collective_id=0, has_side_effects=True, vmem_limit_bytes=56 * 2**20),
         name="conv_stats",

time: 36.4 us -> 34.1 us (0.937)
  the two profiles are of different devices: /device:TPU:1 before, /device:TPU:64 now
where the time goes in v3:
time: 34.1 us; the launch traced here: 34 us
  Pallas kernels  33.8 us (99%)
    pallas_call x1, Pallas kernels, shards(): pl.pallas_call(conv_kernel, out_shape=(pltpu.VMEM((FR, 4, 256, 256), F32)...  32.1 us
    pallas_call x1, Pallas kernels, shards(): pl.pallas_call(norm_kernel, out_shape=jax.ShapeDtypeStruct((FR, ROWS, COL...  1.67 us

profile of v3, /device:TPU:64, one launch (start us, length us, event | category | flops | bytes accessed | tf_op | source)
XLA Modules:
  0.0 34.0 jit_solution(5008961014349272681)
XLA Ops:
  0.0 0.0 copy-start.1
  0.0 0.0 copy-start
  0.0 32.1 %conv_stats.1 = (f32[4,4,256,256]{3,2,1,0:T(8,128)S(1)}, f32[8,128]{1,0:T(8,128)S(1)}) custom-call(bf16[4,8,256,128]{3,2,1,0:T(8,128)(2,1)} %x.1, bf16[3,1152,128]{2,1,0:T(8,128)(2,1)} %w.1, s32[32]{0:T(128)} %lens_hbm.1), custom_call_target="tpu_custom_call" | custom-call | tf_op jit(solution)/shard_map/conv_stats/pallas_call | solution.py:379
  32.1 0.0 copy-done.1
  32.1 0.0 copy-done
  32.1 1.7 %normalize.1 = bf16[4,8,256,128]{3,2,1,0:T(8,128)(2,1)} custom-call(f32[4,4,256,256]{3,2,1,0:T(8,128)S(1)} %get-tuple-element.7.acc, f32[8,128]{1,0:T(8,128)S(1)} %get-tuple-element.8.tab, f32[1,128]{1,0:T(1,128)S(1)} %bitcast.2, f32[1,128]{1,0:T(1,128)S(1)} %bitcast.3), custom_call_target="tpu_custom_call" | custom-call | tf_op jit(solution)/shard_map/normalize/pallas_call | solution.py:396
Async XLA Ops:
  0.0 32.1 %copy-start.1 = (f32[128]{0:T(128)S(1)}, f32[128]{0:T(128)}, u32[]{:S(2)}) copy-start(f32[128]{0:T(128)} %param.8) | copy-start | bytes 1540
  0.0 32.1 %copy-start = (f32[128]{0:T(128)S(1)}, f32[128]{0:T(128)}, u32[]{:S(2)}) copy-start(f32[128]{0:T(128)} %param.7) | copy-start | bytes 1540

commit v4 on v3

--- a/solution.py
+++ b/solution.py
@@ -84,7 +84,7 @@
     lens_load.start()
     loads = [pltpu.make_async_copy(x.at[f], XL.at[f], lsem.at[f]) for f in range(FR)]
     wloads = [pltpu.make_async_copy(w.at[lag], W.at[lag, pl.ds(0, 1152), pl.ds(0, 128)], wsem.at[lag]) for lag in range(3)]
-    for c in [loads[0]] + wloads + loads[1:]:
+    for c in (loads[0], wloads[0], loads[1], wloads[1], loads[2], wloads[2], loads[3]):
         c.start()
 
     for lag in range(3):
@@ -98,12 +98,12 @@
 
     xc = []
     for i, (r0, n) in enumerate([(0, 1), (7, 1), (1, 2), (3, 2), (5, 2)]):
-        xc.append(rcopy(x.at[pl.ds(2, 2), pl.ds(r0, n)], XH.at[:, pl.ds(r0, n)], xsem_s.at[i], xsem_r.at[i], nxt))
+        xc.append(rcopy(x.at[pl.ds(2, 2), pl.ds(r0, n)], XH.at[:, pl.ds(r0, n)], xsem_s, xsem_r.at[i], nxt))
     yc = [
-        rcopy(x.at[:, 7], YU.at[pl.ds(2, 4)], ysem_s.at[0], ysem_r.at[0], up),
-        rcopy(x.at[:, 0], YD.at[pl.ds(2, 4)], ysem_s.at[1], ysem_r.at[1], down),
-        rcopy(XH.at[:, 7], YU.at[pl.ds(0, 2)], ysem_s.at[2], ysem_r.at[2], up),
-        rcopy(XH.at[:, 0], YD.at[pl.ds(0, 2)], ysem_s.at[3], ysem_r.at[3], down),
+        rcopy(x.at[:, 7], YU.at[pl.ds(2, 4)], ysem_s, ysem_r.at[0], up),
+        rcopy(x.at[:, 0], YD.at[pl.ds(2, 4)], ysem_s, ysem_r.at[1], down),
+        rcopy(XH.at[:, 7], YU.at[pl.ds(0, 2)], ysem_s, ysem_r.at[2], up),
+        rcopy(XH.at[:, 0], YD.at[pl.ds(0, 2)], ysem_s, ysem_r.at[3], down),
     ]
     @pl.when(has_next)
     def _():
@@ -128,7 +128,6 @@
             for c in copies:
                 c.wait_recv()
 
-    greet(tok, direct)
 
     lens_load.wait()
     pos = [t * FR + i for i in range(FR)]
@@ -153,13 +152,14 @@
     def dot(a, b):
         return jnp.dot(a, b, preferred_element_type=F32)
 
-    for c in loads:
-        c.wait()
+    loads[0].wait()
     build(0)
-    for lag in range(3):
-        wloads[lag].wait()
-        W[lag, 384:1536, 128:256] = W[lag, 0:1152, 0:128]
     for f in range(FR):
+        if f + 1 < FR:
+            loads[f + 1].wait()
+        if f < 3:
+            wloads[f].wait()
+            W[f, 384:1536, 128:256] = W[f, 0:1152, 0:128]
         tot = None
         for lag in range(min(f, 2), -1, -1):
             a = PA[f + 2 - lag, 1:4].reshape(768, 768)
@@ -176,12 +176,14 @@
         acc[f, 3] = d0[2]
         if f + 1 < FR:
             build(f + 1)
-        if f == 1:
-            pl.semaphore_wait(tok, count(direct))
-            greet(tok2, second)
+        if f == 0:
+            greet(tok, direct)
+        if f == 2:
             landed(xc[0], xc[1])
             yc[2].start()
             yc[3].start()
+            pl.semaphore_wait(tok, count(direct))
+            greet(tok2, second)
 
     def stat(i, k):
         v = acc[i, k]
@@ -283,22 +285,20 @@
     buf1[core * S + y] = mine
 
     s1 = []
-    for i, (dc, dy) in enumerate(near):
-        s1.append(rcopy(st, buf1.at[core * S + y], s1_s.at[i], s1_r.at[i], near_dev(dc, dy)))
+    for dc, dy in near:
+        s1.append(rcopy(st, buf1.at[core * S + y], s1_s, s1_r, near_dev(dc, dy)))
     pl.semaphore_wait(tok2, count(second))
     for c in s1:
         c.start()
 
     @pl.when(has_next)
     def _():
-        for c in xc:
-            c.wait_send()
-
-    for c in yc:
-        c.wait_send()
+        rcopy(XH, XH, xsem_s, xsem_r.at[0], nxt).wait_send()
+
+    rcopy(x.at[:, pl.ds(0, 3)], x.at[:, pl.ds(0, 3)], ysem_s, ysem_r.at[0], up).wait_send()
     weight = [1.0 / (jnp.full((1, 128), 1.0, F32) * (ends[i] - starts[i]).astype(F32)) for i in range(FR)]
-    for c in s1:
-        c.wait_recv()
+    s1_all = rcopy(buf1.at[pl.ds(0, 7)], buf1.at[pl.ds(0, 7)], s1_s, s1_r, near_dev(1, 0))
+    s1_all.wait_recv()
 
     parts = []
     for c in range(2):
@@ -312,22 +312,26 @@
     buf2[2 * NX + cx] = chip_table
 
     s2 = {}
-    for i, (dz, dx) in enumerate(far):
-        c = rcopy(ct, buf2.at[(2 - dz) * NX + cx], s2_s.at[i], s2_r.at[i], far_dev(dz, dx))
+    for dz, dx in far:
+        c = rcopy(ct, buf2.at[(2 - dz) * NX + cx], s2_s.at[dz + 2], s2_r.at[dz + 2], far_dev(dz, dx))
         s2.setdefault(dz, []).append(c)
 
-    def each(dz, there, act):
-        def run():
-            for c in s2[dz]:
-                act(c)
-        pl.when(has_z(there))(run)
+    def start(dz):
+        for c in s2[dz]:
+            c.start()
+
+    def whole(dz):
+        part = buf2.at[pl.ds(0, len(s2[dz]))]
+        return rcopy(part, part, s2_s.at[dz + 2], s2_r.at[dz + 2], near_dev(1, 0))
+
+    def on(cond, act, *a):
+        pl.when(cond)(lambda: act(*a))
 
     for dz in s2:
-        each(dz, dz, lambda c: c.start())
-    for c in s1:
-        c.wait_send()
+        on(has_z(dz), start, dz)
+    s1_all.wait_send()
     for dz in s2:
-        each(dz, -dz, lambda c: c.wait_recv())
+        on(has_z(-dz), lambda dz: whole(dz).wait_recv(), dz)
 
     shape = (5 * NX, 8, 128)
     frame = ((cz - 2) * NX + lax.broadcasted_iota(jnp.int32, shape, 0)) * 8 + lax.broadcasted_iota(jnp.int32, shape, 1)
@@ -347,7 +351,7 @@
     tab[...] = jnp.where(row8 < 4, both, lax.rsqrt(both + 1e-6))
 
     for dz in s2:
-        each(dz, dz, lambda c: c.wait_send())
+        on(has_z(dz), lambda dz: whole(dz).wait_send(), dz)
 
 
 def norm_kernel(acc, tab, gain, shift, out, buf, sem):
@@ -388,7 +392,7 @@
             V((4, 4, 256), F32), V((4, 4, 256), F32), V((4, 128), F32), V((8, 128), F32),
             V((8, 4, 128), F32), V((20, 8, 128), F32),
             D, pltpu.SemaphoreType.REGULAR, pltpu.SemaphoreType.REGULAR,
-            D((4,)), D((3,)), D((5,)), D((5,)), D((4,)), D((4,)), D((7,)), D((7,)), D((19,)), D((19,)),
+            D((4,)), D((3,)), D, D((5,)), D, D((4,)), D, D, D((5,)), D((5,)),
         ],
         compiler_params=pltpu.CompilerParams(collective_id=0, has_side_effects=True, vmem_limit_bytes=56 * 2**20),
         name="conv_stats",

time: 34.1 us -> 32.9 us (0.965)
  Pallas kernels: 33.8 us -> 32.6 us
    pallas_call x1, Pallas kernels: 32.1 us -> 30.9 us  [shards(): pl.pallas_call(conv_kernel, out_shape=(pltpu.VMEM((FR, 4, 256, 256), F32)...]
where the time goes in v4:
time: 32.9 us; the launch traced here: 32.7 us
  Pallas kernels  32.6 us (99%)
    pallas_call x1, Pallas kernels, shards(): pl.pallas_call(conv_kernel, out_shape=(pltpu.VMEM((FR, 4, 256, 256), F32)...  30.9 us
    pallas_call x1, Pallas kernels, shards(): pl.pallas_call(norm_kernel, out_shape=jax.ShapeDtypeStruct((FR, ROWS, COL...  1.67 us

profile of v4, /device:TPU:64, one launch (start us, length us, event | category | flops | bytes accessed | tf_op | source)
XLA Modules:
  0.0 32.7 jit_solution(11195758082892121119)
XLA Ops:
  0.0 0.0 copy-start.1
  0.0 0.0 copy-start
  0.0 30.9 %conv_stats.1 = (f32[4,4,256,256]{3,2,1,0:T(8,128)S(1)}, f32[8,128]{1,0:T(8,128)S(1)}) custom-call(bf16[4,8,256,128]{3,2,1,0:T(8,128)(2,1)} %x.1, bf16[3,1152,128]{2,1,0:T(8,128)(2,1)} %w.1, s32[32]{0:T(128)} %lens_hbm.1), custom_call_target="tpu_custom_call" | custom-call | tf_op jit(solution)/shard_map/conv_stats/pallas_call | solution.py:383
  30.9 0.0 copy-done.1
  30.9 0.0 copy-done
  30.9 1.7 %normalize.1 = bf16[4,8,256,128]{3,2,1,0:T(8,128)(2,1)} custom-call(f32[4,4,256,256]{3,2,1,0:T(8,128)S(1)} %get-tuple-element.7.acc, f32[8,128]{1,0:T(8,128)S(1)} %get-tuple-element.8.tab, f32[1,128]{1,0:T(1,128)S(1)} %bitcast.2, f32[1,128]{1,0:T(1,128)S(1)} %bitcast.3), custom_call_target="tpu_custom_call" | custom-call | tf_op jit(solution)/shard_map/normalize/pallas_call | solution.py:400
Async XLA Ops:
  0.0 30.9 %copy-start.1 = (f32[128]{0:T(128)S(1)}, f32[128]{0:T(128)}, u32[]{:S(2)}) copy-start(f32[128]{0:T(128)} %param.8) | copy-start | bytes 1540
  0.0 30.9 %copy-start = (f32[128]{0:T(128)S(1)}, f32[128]{0:T(128)}, u32[]{:S(2)}) copy-start(f32[128]{0:T(128)} %param.7) | copy-start | bytes 1540

commit v5 on v4

--- a/solution.py
+++ b/solution.py
@@ -64,6 +64,7 @@
               (far_dev(1, 0), has_z(1)), (far_dev(-1, 0), has_z(-1))]
     second = [(far_dev(2, 0), has_z(2)), (far_dev(-2, 0), has_z(-2)), (far_dev(1, 0), has_z(1)), (far_dev(-1, 0), has_z(-1)),
               (near_dev(1, 0), None)]
+    first = [(down, None), (far_dev(0, 3), None), (far_dev(1, 0), has_z(1)), (far_dev(-1, 0), has_z(-1))]
     barrier = pltpu.get_barrier_semaphore()
 
     def greet(sem, devices):
@@ -78,15 +79,15 @@
     def count(devices):
         return sum(jnp.int32(1) if cond is None else cond.astype(jnp.int32) for _, cond in devices)
 
+    loads = [pltpu.make_async_copy(x.at[f], XL.at[f], lsem.at[f]) for f in range(FR)]
+    wloads = [pltpu.make_async_copy(w.at[lag], W.at[lag, pl.ds(0, 1152), pl.ds(0, 128)], wsem.at[lag]) for lag in range(3)]
+    lens_load = pltpu.make_async_copy(lens_hbm, lens, lensem)
+    for c in (lens_load, loads[0], wloads[0]):
+        c.start()
     buf2[...] = jnp.zeros_like(buf2)
     greet(barrier, direct)
-    lens_load = pltpu.make_async_copy(lens_hbm, lens, lensem)
-    lens_load.start()
-    loads = [pltpu.make_async_copy(x.at[f], XL.at[f], lsem.at[f]) for f in range(FR)]
-    wloads = [pltpu.make_async_copy(w.at[lag], W.at[lag, pl.ds(0, 1152), pl.ds(0, 128)], wsem.at[lag]) for lag in range(3)]
-    for c in (loads[0], wloads[0], loads[1], wloads[1], loads[2], wloads[2], loads[3]):
+    for c in (loads[1], wloads[1], loads[2], wloads[2], loads[3]):
         c.start()
-
     for lag in range(3):
         W[lag, 1152:1536, 0:128] = jnp.zeros((384, 128), BF)
         W[lag, 0:384, 128:256] = jnp.zeros((384, 128), BF)
@@ -132,16 +133,12 @@
     lens_load.wait()
     pos = [t * FR + i for i in range(FR)]
 
-    def bounds(k, c):
-        cum, starts, ends = c
-        after = cum + lens[k]
-        inside = [(cum <= p) & (p < after) for p in pos]
-        starts = tuple(jnp.where(i, cum, s) for i, s in zip(inside, starts))
-        ends = tuple(jnp.where(i, after, e) for i, e in zip(inside, ends))
-        return after, starts, ends
+    def begin(k, c):
+        cum, starts = c
+        return cum + lens[k], tuple(jnp.where(cum <= p, cum, a) for p, a in zip(pos, starts))
 
     zero = jnp.int32(0)
-    _, starts, ends = lax.fori_loop(0, 32, bounds, (zero, (zero,) * FR, (zero,) * FR))
+    _, starts = lax.fori_loop(0, 32, begin, (zero, (zero,) * FR), unroll=4)
     within = [[jnp.where(pos[i] - lag >= starts[i], 1.0, 0.0).astype(F32) for lag in range(3)] for i in range(FR)]
 
     def build(f):
@@ -177,12 +174,12 @@
         if f + 1 < FR:
             build(f + 1)
         if f == 0:
-            greet(tok, direct)
+            greet(tok, first)
         if f == 2:
             landed(xc[0], xc[1])
             yc[2].start()
             yc[3].start()
-            pl.semaphore_wait(tok, count(direct))
+            pl.semaphore_wait(tok, count(first))
             greet(tok2, second)
 
     def stat(i, k):
@@ -296,6 +293,12 @@
         rcopy(XH, XH, xsem_s, xsem_r.at[0], nxt).wait_send()
 
     rcopy(x.at[:, pl.ds(0, 3)], x.at[:, pl.ds(0, 3)], ysem_s, ysem_r.at[0], up).wait_send()
+    def finish(k, c):
+        cum, ends = c
+        after = cum + lens[k]
+        return after, tuple(jnp.where(cum <= p, after, a) for p, a in zip(pos, ends))
+
+    _, ends = lax.fori_loop(0, 32, finish, (zero, (zero,) * FR), unroll=4)
     weight = [1.0 / (jnp.full((1, 128), 1.0, F32) * (ends[i] - starts[i]).astype(F32)) for i in range(FR)]
     s1_all = rcopy(buf1.at[pl.ds(0, 7)], buf1.at[pl.ds(0, 7)], s1_s, s1_r, near_dev(1, 0))
     s1_all.wait_recv()
@@ -330,6 +333,8 @@
     for dz in s2:
         on(has_z(dz), start, dz)
     s1_all.wait_send()
+    for dz in s2:
+        on(has_z(dz), lambda dz: whole(dz).wait_send(), dz)
     for dz in s2:
         on(has_z(-dz), lambda dz: whole(dz).wait_recv(), dz)
 
@@ -349,9 +354,6 @@
     row8 = lax.broadcasted_iota(jnp.int32, (8, 128), 0)
     both = group_sum(jnp.where(lane8 == jnp.where(row8 < 4, 0, 1), both, 0.0))
     tab[...] = jnp.where(row8 < 4, both, lax.rsqrt(both + 1e-6))
-
-    for dz in s2:
-        on(has_z(dz), lambda dz: whole(dz).wait_send(), dz)
 
 
 def norm_kernel(acc, tab, gain, shift, out, buf, sem):

time: 32.9 us -> 32.8 us (level)
  no operation moved by 1% of the time
where the time goes in v5:
time: 32.8 us; the launch traced here: 32.7 us
  Pallas kernels  32.5 us (99%)
    pallas_call x1, Pallas kernels, shards(): pl.pallas_call(conv_kernel, out_shape=(pltpu.VMEM((FR, 4, 256, 256), F32)...  30.9 us
    pallas_call x1, Pallas kernels, shards(): pl.pallas_call(norm_kernel, out_shape=jax.ShapeDtypeStruct((FR, ROWS, COL...  1.67 us

profile of v5, /device:TPU:64, one launch (start us, length us, event | category | flops | bytes accessed | tf_op | source)
XLA Modules:
  0.0 32.7 jit_solution(17744407896858183654)
XLA Ops:
  0.0 0.0 copy-start.1
  0.0 0.0 copy-start
  0.0 30.9 %conv_stats.1 = (f32[4,4,256,256]{3,2,1,0:T(8,128)S(1)}, f32[8,128]{1,0:T(8,128)S(1)}) custom-call(bf16[4,8,256,128]{3,2,1,0:T(8,128)(2,1)} %x.1, bf16[3,1152,128]{2,1,0:T(8,128)(2,1)} %w.1, s32[32]{0:T(128)} %lens_hbm.1), custom_call_target="tpu_custom_call" | custom-call | tf_op jit(solution)/shard_map/conv_stats/pallas_call | solution.py:385
  30.9 0.0 copy-done.1
  30.9 0.0 copy-done
  30.9 1.7 %normalize.1 = bf16[4,8,256,128]{3,2,1,0:T(8,128)(2,1)} custom-call(f32[4,4,256,256]{3,2,1,0:T(8,128)S(1)} %get-tuple-element.7.acc, f32[8,128]{1,0:T(8,128)S(1)} %get-tuple-element.8.tab, f32[1,128]{1,0:T(1,128)S(1)} %bitcast.2, f32[1,128]{1,0:T(1,128)S(1)} %bitcast.3), custom_call_target="tpu_custom_call" | custom-call | tf_op jit(solution)/shard_map/normalize/pallas_call | solution.py:402
Async XLA Ops:
  0.0 30.9 %copy-start.1 = (f32[128]{0:T(128)S(1)}, f32[128]{0:T(128)}, u32[]{:S(2)}) copy-start(f32[128]{0:T(128)} %param.8) | copy-start | bytes 1540
  0.0 30.9 %copy-start = (f32[128]{0:T(128)S(1)}, f32[128]{0:T(128)}, u32[]{:S(2)}) copy-start(f32[128]{0:T(128)} %param.7) | copy-start | bytes 1540

commit v6 on v5

--- a/solution.py
+++ b/solution.py
@@ -252,15 +252,17 @@
         rims(f, 0)
     early(0)
     early(4)
+    stat(0, 0)
+    stat(1, 0)
     landed(xc[3])
     early_rows(2)
     early(2)
-    stat(0, 0)
-    stat(1, 0)
+    stat(0, 1)
+    stat(1, 1)
     landed(xc[4])
     early_rows(3)
     early(3)
-    for i, k in ((0, 1), (1, 1), (0, 2), (1, 2), (0, 3), (1, 3)):
+    for i, k in ((0, 2), (1, 2), (0, 3), (1, 3)):
         stat(i, k)
 
     lane = lax.broadcasted_iota(jnp.int32, (FR, 128), 1) % 4

time: 32.8 us -> 32.7 us (level)
  no operation moved by 1% of the time
where the time goes in v6:
time: 32.7 us
  Pallas kernels  32.5 us (99%)
    pallas_call x1, Pallas kernels, shards(): pl.pallas_call(conv_kernel, out_shape=(pltpu.VMEM((FR, 4, 256, 256), F32)...  30.8 us
    pallas_call x1, Pallas kernels, shards(): pl.pallas_call(norm_kernel, out_shape=jax.ShapeDtypeStruct((FR, ROWS, COL...  1.67 us

profile of v6, /device:TPU:64, one launch (start us, length us, event | category | flops | bytes accessed | tf_op | source)
XLA Modules:
  0.0 32.7 jit_solution(16713050347566750049)
XLA Ops:
  0.0 0.0 copy-start.1
  0.0 0.0 copy-start
  0.0 30.8 %conv_stats.1 = (f32[4,4,256,256]{3,2,1,0:T(8,128)S(1)}, f32[8,128]{1,0:T(8,128)S(1)}) custom-call(bf16[4,8,256,128]{3,2,1,0:T(8,128)(2,1)} %x.1, bf16[3,1152,128]{2,1,0:T(8,128)(2,1)} %w.1, s32[32]{0:T(128)} %lens_hbm.1), custom_call_target="tpu_custom_call" | custom-call | tf_op jit(solution)/shard_map/conv_stats/pallas_call | solution.py:387
  30.8 0.0 copy-done.1
  30.8 0.0 copy-done
  30.8 1.7 %normalize.1 = bf16[4,8,256,128]{3,2,1,0:T(8,128)(2,1)} custom-call(f32[4,4,256,256]{3,2,1,0:T(8,128)S(1)} %get-tuple-element.7.acc, f32[8,128]{1,0:T(8,128)S(1)} %get-tuple-element.8.tab, f32[1,128]{1,0:T(1,128)S(1)} %bitcast.2, f32[1,128]{1,0:T(1,128)S(1)} %bitcast.3), custom_call_target="tpu_custom_call" | custom-call | tf_op jit(solution)/shard_map/normalize/pallas_call | solution.py:404
Async XLA Ops:
  0.0 30.8 %copy-start.1 = (f32[128]{0:T(128)S(1)}, f32[128]{0:T(128)}, u32[]{:S(2)}) copy-start(f32[128]{0:T(128)} %param.8) | copy-start | bytes 1540
  0.0 30.8 %copy-start = (f32[128]{0:T(128)S(1)}, f32[128]{0:T(128)}, u32[]{:S(2)}) copy-start(f32[128]{0:T(128)} %param.7) | copy-start | bytes 1540
